TPU v7x, 128 devices: a whole 4x4x4 slice. The times are simulated.
128 devices in a mesh: atm: 8 (over x, core), ice: 16 (over y, z).
Axes of the slice: x: 4, y: 4, z: 4, core: 2. Of those that a mesh axis runs over, the one named last changes fastest.
Arguments:
- atmospheric_driver: float32 [8, 1310720], P(None, ('atm', 'ice')), may hold values from 0 to 1
- dispatcher_own_records: int32 [8388608], P(('atm', 'ice')), may hold values from -1 to 10239, as said below
- overlay_holder_position: int32 [4, 2097152], P(None, ('atm', 'ice')), may hold values from 0 to 65535, as said below
- overlay_regrid_factor: float32 [4, 2097152], P(None, ('atm', 'ice')), may hold values from 0.05 to 0.5
- thermal_excess: float32 [30, 2097152], P(None, ('atm', 'ice')), may hold values from -1 to 0
- meltwater: float32 [30, 2097152], P(None, ('atm', 'ice')), may hold values from 0 to 0.3
- snowpack_compactness: float32 [30, 2097152], P(None, ('atm', 'ice')), may hold values from 0.3 to 0.9
- retention_limit: float32 [30, 2097152], P(None, ('atm', 'ice')), may hold values from 0.05 to 0.5
Outputs:
- class_balance: float32 [1310720], P(('atm', 'ice'))
- class_albedo: float32 [1310720], P(('atm', 'ice'))
- thermal_after_hour: float32 [30, 2097152], P(None, ('atm', 'ice'))
- meltwater_after_hour: float32 [30, 2097152], P(None, ('atm', 'ice'))
Inputs may be any that keep to these rules, and one draw needn't show every extreme that they name: `dispatcher_own_records`: live entries are local rows of the sender (0 to 10239); the rest are -1, and in each (sending block, receiving block) pair the live entries come first. Write an owner's block index as atm index times the size of the ice axis plus ice index. Block b takes live slots only from four senders, each with at least one live slot: b itself, the two owners with the same atm index and ice index one lower and one higher (wrapping around), and the owner with the same ice index and atm index half the size of the atm axis further on (wrapping around); every other pair has none. `overlay_holder_position`: every intersection names a live slot: index s * 512 + slot with dispatcher_own_records[s, b, slot] not -1, b the cell's block.
All inputs are finite; a program needn't handle non-finite values.
Results may differ from a plain program's by a relative error of at most 0.0003.
Values sent between devices are 32-bit elements; how exact they have to be, the bound alone decides.
No kernel may reach another device: no remote copies, remote signals or barrier semaphores. Data moves between devices by JAX's collectives and lax.ppermute only.
A program may use at most 64 MiB of HBM per device.

v0:
```python
import functools

import jax
import jax.numpy as jnp
from jax import lax
from jax.experimental import pallas as pl
from jax.experimental.pallas import tpu as pltpu
from jax.sharding import PartitionSpec as P

DIFFUSION_ITERS = 4
PERCOLATE_ROUNDS = 6
LANES = 128
TILE = 1024
F32 = jnp.float32
BF16 = jnp.bfloat16
VMEM_SMALL = 8 << 20
VMEM_LARGE = 62 << 20
VMEM_MOST = 65280 << 10


def kernel_params(limit):
    return pltpu.CompilerParams(vmem_limit_bytes=limit)


def partner_ids(atm_count, ice_count):
    a = lax.axis_index("atm")
    i = lax.axis_index("ice")
    even = i ^ 1
    odd = lax.rem(((i + ice_count - 1) ^ 1) + 1, ice_count)
    far = lax.rem(a + atm_count // 2, atm_count)
    return (
        a * ice_count + i,
        a * ice_count + even,
        a * ice_count + odd,
        far * ice_count + i,
    )


def spread(row):
    return jnp.broadcast_to(row, (8, LANES))


def pick_kernel(mesh_shape, records, driver_any, o0, o1, o2, o3, index_out, driver, index, sems):
    ids = partner_ids(*mesh_shape)
    copies = [pltpu.make_async_copy(driver_any, driver, sems.at[4])]
    for place in range(4):
        copies.append(
            pltpu.make_async_copy(records.at[ids[place]], index.at[place], sems.at[place])
        )
    for copy in copies:
        copy.start()
    for copy in copies:
        copy.wait()
    fields, rows = driver.shape
    per_place = index.shape[1]
    for place, out in enumerate((o0, o1, o2, o3)):
        block = index[place]
        for j in range(per_place):
            row = block[j : j + 1, :]
            index_out[place * per_place + j : place * per_place + j + 1, :] = row
            where = spread(row)
            low = where & (LANES - 1)
            high = where >> 7
            total = jnp.zeros((fields, LANES), F32)
            for c in range(rows // LANES):
                found = jnp.take_along_axis(
                    driver[:, c * LANES : (c + 1) * LANES], low, axis=1
                )
                total = jnp.where(high == c, found, total)
            out[:, j * LANES : (j + 1) * LANES] = total


def pick_rows(mesh_shape, records, driver):
    fields = driver.shape[0]
    per_place = records.shape[1]
    slots = per_place * LANES
    vmem = pl.BlockSpec(memory_space=pltpu.VMEM)
    return pl.pallas_call(
        functools.partial(pick_kernel, mesh_shape),
        out_shape=[jax.ShapeDtypeStruct((fields, slots), F32)] * 4
        + [jax.ShapeDtypeStruct((4 * per_place, LANES), jnp.int32)],
        in_specs=[pl.BlockSpec(memory_space=pl.ANY)] * 2,
        out_specs=[vmem] * 5,
        scratch_shapes=[
            pltpu.VMEM(driver.shape, F32),
            pltpu.VMEM((4, per_place, LANES), jnp.int32),
            pltpu.SemaphoreType.DMA((5,)),
        ],
        compiler_params=kernel_params(VMEM_MOST),
        name="pick_rows",
    )(records, driver)


def to_layers(block, scratch, column, layers):
    for i in range(0, layers, 8):
        height = min(8, layers - i)
        for j in range(8):
            scratch[pl.ds(i * 8 + j * 8, height), :] = block[
                pl.ds(i, height), pl.ds(column + j * LANES, LANES)
            ]


def from_layers(block, scratch, column, layers):
    for i in range(0, layers, 8):
        height = min(8, layers - i)
        for j in range(8):
            block[pl.ds(i, height), pl.ds(column + j * LANES, LANES)] = scratch[
                pl.ds(i * 8 + j * 8, height), :
            ]


def layer(scratch, l):
    return scratch[pl.ds((l // 8) * 64 + l % 8, 8, stride=8), :]


def put_layer(scratch, l, value):
    scratch[pl.ds((l // 8) * 64 + l % 8, 8, stride=8), :] = value


class Conduct:
    def __init__(self, low, layers):
        self.low = low
        self.layers = layers
        self.temps = [dict() for _ in range(DIFFUSION_ITERS + 1)]
        self.flows = [dict() for _ in range(DIFFUSION_ITERS + 1)]
        self.between = {}
        self.conductance = {}

    def add(self, l, temp, density):
        self.temps[0][l] = temp
        self.conductance[l] = 0.2 + 0.25 * density
        if l > self.low:
            self.between[l - 1] = 0.5 * (self.conductance[l] + self.conductance[l - 1])
        for s in range(1, DIFFUSION_ITERS + 1):
            self.sweep(s, l - s)
        if l == self.layers - 1:
            for extra in range(1, DIFFUSION_ITERS + 1):
                for s in range(1, DIFFUSION_ITERS + 1):
                    self.sweep(s, l + extra - s)

    def sweep(self, s, m):
        before = self.temps[s - 1]
        bottom = m == self.layers - 1
        if m in self.temps[s] or m not in before:
            return
        if not bottom:
            if m + 1 not in before or m not in self.between:
                return
            self.flows[s][m] = self.between[m] * (before[m + 1] - before[m])
        if m > 0 and (m - 1) not in self.flows[s]:
            return
        value = before[m]
        if not bottom:
            value = value + self.flows[s][m]
        if m > 0:
            value = value - self.flows[s][m - 1]
        self.temps[s][m] = value


class Column:
    def __init__(self, temp, water, limit):
        self.half = -0.5 * temp
        self.water = water
        self.limit = limit
        self.leaving = {}

    def leave(self, r):
        held = jnp.minimum(self.water, self.limit)
        self.leaving[r] = self.water - held
        return held

    def round(self, r, arriving):
        held = self.leave(r)
        if arriving is not None:
            held = held + arriving
        frozen = jnp.minimum(held, jnp.maximum(self.half, 0.0))
        self.water = held - frozen
        self.half = self.half - 0.75 * frozen


def deep_steps(st, sw, sd, sl, ot, ow, layers, found):
    reach = DIFFUSION_ITERS
    conduct = Conduct(1, layers)
    columns = {}
    ready = reach
    for l in range(1, layers):
        conduct.add(l, layer(st, l), layer(sd, l))
        yield
        while ready < layers and (ready == reach or ready in conduct.temps[reach]):
            m = ready
            ready += 1
            if m == reach:
                columns[m] = Column(jnp.zeros((8, LANES), F32), layer(sw, m), layer(sl, m))
                columns[m].leave(0)
                continue
            column = Column(conduct.temps[reach][m], layer(sw, m), layer(sl, m))
            columns[m] = column
            rounds = min(m - reach, PERCOLATE_ROUNDS)
            for r in range(rounds):
                column.round(r, columns[m - 1].leaving[r])
                yield
            if rounds < PERCOLATE_ROUNDS:
                column.leave(rounds)
            else:
                put_layer(ot, m, -2.0 * column.half)
                put_layer(ow, m, column.water)
            if m - 1 >= reach + PERCOLATE_ROUNDS:
                del columns[m - 1]
            yield
    last = columns[layers - 1].leaving
    runoff = last[0]
    for r in range(1, PERCOLATE_ROUNDS):
        runoff = runoff + last[r]
    found["runoff"] = runoff
    found["columns"] = columns


def upper_steps(st, sw, sd, sl, ot, ow, top, gain, columns):
    reach = DIFFUSION_ITERS
    conduct = Conduct(0, 1 << 20)
    above = None
    for l in range(2 * reach + 1):
        conduct.add(l, top if l == 0 else layer(st, l), layer(sd, l))
        yield
        m = l - reach
        if m < 0:
            continue
        water = layer(sw, m)
        if m == 0:
            water = water + gain
        column = Column(conduct.temps[reach][m], water, layer(sl, m))
        for r in range(PERCOLATE_ROUNDS):
            column.round(r, None if above is None else above.leaving[r])
            yield
        put_layer(ot, m, -2.0 * column.half)
        put_layer(ow, m, column.water)
        above = column
    for m in range(reach + 1, reach + PERCOLATE_ROUNDS):
        column = columns[m]
        for r in range(m - reach, PERCOLATE_ROUNDS):
            column.round(r, above.leaving[r])
            yield
        put_layer(ot, m, -2.0 * column.half)
        put_layer(ow, m, column.water)
        above = column


def together(main, beside, each):
    going = True
    for _ in main:
        for _ in range(each):
            if going:
                going = next(beside, False) is None
    for _ in beside:
        pass


def two_terms(value):
    first = value.astype(BF16).astype(F32)
    return first, value - first


def gather_steps(table, low, high, weights, fields, chunks, forced):
    for k in range(len(low)):
        found = [jnp.zeros((8, LANES), F32) for _ in range(fields)]
        for c in range(chunks):
            here = high[k] == c
            for f in range(fields):
                value = jnp.take_along_axis(
                    table[pl.ds((c * fields + f) * 8, 8), :], low[k], axis=1
                )
                found[f] = jnp.where(here, value, found[f])
            yield
        for f in range(fields):
            part = found[f] * weights[k]
            forced[f] = part if k == 0 else forced[f] + part


def packed(row):
    return jnp.broadcast_to(row, (16, LANES)).astype(BF16)


def sixteens(count):
    base = lax.broadcasted_iota(jnp.int32, (16, LANES), 0)
    return [(base + 16 * j).astype(F32).astype(BF16) for j in range(count // 16)]


def scatter_steps(total, low, high, weights, values, chunks):
    one = jnp.ones((16, LANES), BF16)
    zero = jnp.zeros((16, LANES), BF16)
    lane_numbers = sixteens(LANES)
    chunk_numbers = sixteens(chunks)
    for k in range(len(low)):
        terms = [t for v in values for t in two_terms(v * weights[k])]
        low_f = low[k].astype(F32)
        high_f = high[k].astype(F32)
        lefts = []
        rights = []
        for s in range(8):
            low_row = packed(low_f[s : s + 1, :])
            high_row = packed(high_f[s : s + 1, :])
            rights.append(
                jnp.concatenate([jnp.where(low_row == n, one, zero) for n in lane_numbers], 0)
            )
            here = [high_row == n for n in chunk_numbers]
            parts = []
            for term in terms:
                row = packed(term[s : s + 1, :])
                parts += [jnp.where(h, row, zero) for h in here]
            lefts.append(jnp.concatenate(parts, 0))
            yield
        total[...] += lax.dot_general(
            jnp.concatenate(rights, 1),
            jnp.concatenate(lefts, 1),
            (((1,), (1,)), ((), ())),
            preferred_element_type=F32,
        )


def cell_kernel(mesh_shape, *refs):
    position, weight, temp, water, density, limit, t0, t1, t2, t3 = refs[:10]
    o0, o1, o2, o3, temp_out, water_out = refs[10:16]
    table, total, st, sw, sd, sl, ot, ow = refs[16:]
    fields, slots = t0.shape
    per_place = slots // LANES
    chunks = 4 * per_place
    layers, width = temp.shape
    ids = partner_ids(*mesh_shape)

    @pl.when(pl.program_id(0) == 0)
    def _():
        for c in range(chunks):
            piece = (t0, t1, t2, t3)[c // per_place]
            j = c % per_place
            for f in range(fields):
                table[pl.ds((c * fields + f) * 8, 8), :] = spread(
                    piece[f : f + 1, j * LANES : (j + 1) * LANES]
                )
        total[...] = jnp.zeros(total.shape, F32)

    @pl.loop(0, width // TILE)
    def _(tile):
        column = pl.multiple_of(tile * TILE, TILE)
        low = []
        high = []
        weights = []
        for k in range(4):
            rows = pl.ds(tile * 32 + k, 8, stride=4)
            p = position[rows, :]
            owner = p >> (slots.bit_length() - 1)
            place = jnp.zeros((8, LANES), jnp.int32)
            for n in range(1, 4):
                place = jnp.where(owner == ids[n], n, place)
            low.append(p & (LANES - 1))
            high.append(place * per_place + ((p & (slots - 1)) >> 7))
            weights.append(weight[rows, :])
        to_layers(temp, st, column, layers)
        to_layers(density, sd, column, layers)
        to_layers(water, sw, column, layers)
        to_layers(limit, sl, column, layers)
        forced = [None] * fields
        firn = {}
        together(
            gather_steps(table, low, high, weights, fields, chunks, forced),
            deep_steps(st, sw, sd, sl, ot, ow, layers, firn),
            4,
        )
        air = 2.0 * forced[0] - 1.0
        short, long, snow, rain, humid, wind, press = forced[1:]
        albedo = 0.45 + 0.4 * snow / (snow + 0.1) - 0.1 * jnp.maximum(air, 0.0)
        skin = layer(st, 0)
        flux = (
            1.5 * (1.0 - albedo) * short
            + 0.6 * (long - 0.5)
            + 0.5 * wind * (air - skin)
            + 0.3 * wind * (humid - press)
        )
        top = skin + 0.5 * flux
        balance = snow + rain - firn["runoff"] - 0.2 * wind * (press - humid)
        together(
            scatter_steps(total, low, high, weights, (balance, albedo), chunks),
            upper_steps(
                st,
                sw,
                sd,
                sl,
                ot,
                ow,
                jnp.minimum(top, 0.0),
                jnp.maximum(top, 0.0) + rain,
                firn["columns"],
            ),
            3,
        )
        from_layers(temp_out, ot, column, layers)
        from_layers(water_out, ow, column, layers)

    @pl.when(pl.program_id(0) == pl.num_programs(0) - 1)
    def _():
        sums = total[...].T
        for q in range(2):
            first = sums[2 * q * chunks : (2 * q + 1) * chunks]
            second = sums[(2 * q + 1) * chunks : (2 * q + 2) * chunks]
            both = first + second
            for c in range(chunks):
                j = c % per_place
                (o0, o1, o2, o3)[c // per_place][q : q + 1, j * LANES : (j + 1) * LANES] = both[
                    c : c + 1, :
                ]


def cell_sums(mesh_shape, position, weight, temp, water, density, limit, tables):
    fields, slots = tables[0].shape
    chunks = 4 * slots // LANES
    layers, cells = temp.shape
    width = min(cells, 2 * TILE)
    firn = pl.BlockSpec((layers, width), lambda g: (0, g))
    flat = pl.BlockSpec((4 * width // LANES, LANES), lambda g: (g, 0))
    table = pl.BlockSpec((fields, slots), lambda g: (0, 0))
    sums = pl.BlockSpec((2, slots), lambda g: (0, 0))
    padded = -(-layers // 8) * 64
    return pl.pallas_call(
        functools.partial(cell_kernel, mesh_shape),
        grid=(cells // width,),
        out_shape=[jax.ShapeDtypeStruct((2, slots), F32)] * 4
        + [jax.ShapeDtypeStruct((layers, cells), F32)] * 2,
        in_specs=[flat] * 2 + [firn] * 4 + [table] * 4,
        out_specs=[sums] * 4 + [firn] * 2,
        scratch_shapes=[
            pltpu.VMEM((chunks * fields * 8, LANES), F32),
            pltpu.VMEM((LANES, 4 * chunks), F32),
        ]
        + [pltpu.VMEM((padded, LANES), F32)] * 6,
        compiler_params=kernel_params(VMEM_LARGE),
        name="cell_sums",
    )(position, weight, temp, water, density, limit, *tables)


def row_kernel(index, p0, p1, p2, p3, balance_out, albedo_out):
    blocks = balance_out.shape[0]
    per_place = index.shape[0] // 4
    one = jnp.ones((16, LANES), BF16)
    zero = jnp.zeros((16, LANES), BF16)
    lane_numbers = sixteens(LANES)
    block_numbers = sixteens(blocks)
    rights = []
    lefts = []
    for place, piece in enumerate((p0, p1, p2, p3)):
        for j in range(per_place):
            n = place * per_place + j
            row = index[n : n + 1, :]
            low_row = packed((row & (LANES - 1)).astype(F32))
            high_row = packed((row >> 7).astype(F32))
            rights.append(
                jnp.concatenate([jnp.where(low_row == m, one, zero) for m in lane_numbers], 0)
            )
            here = [high_row == m for m in block_numbers]
            parts = []
            for q in range(2):
                for term in two_terms(piece[q : q + 1, j * LANES : (j + 1) * LANES]):
                    value = packed(term)
                    parts += [jnp.where(h, value, zero) for h in here]
            lefts.append(jnp.concatenate(parts, 0))
    total = lax.dot_general(
        jnp.concatenate(lefts, 1),
        jnp.concatenate(rights, 1),
        (((1,), (1,)), ((), ())),
        preferred_element_type=F32,
    )
    balance_out[...] = total[:blocks] + total[blocks : 2 * blocks]
    albedo_out[...] = total[2 * blocks : 3 * blocks] + total[3 * blocks :]


def row_sums(index, pieces, rows):
    blocks = rows // LANES
    vmem = pl.BlockSpec(memory_space=pltpu.VMEM)
    return pl.pallas_call(
        row_kernel,
        out_shape=[jax.ShapeDtypeStruct((blocks, LANES), F32)] * 2,
        in_specs=[vmem] * 5,
        out_specs=[vmem] * 2,
        compiler_params=kernel_params(VMEM_SMALL),
        name="row_sums",
    )(index, *pieces)


def lay_flat(array):
    k, cells = array.shape
    return (
        array.reshape(k, cells // LANES, LANES).transpose(1, 0, 2).reshape(k * cells // LANES, LANES)
    )


def ring_partners(ice_count):
    even = [i ^ 1 for i in range(ice_count)]
    odd = [(((i - 1) ^ 1) + 1) % ice_count for i in range(ice_count)]
    return even, odd


def swap_partners(pieces, atm_count, ice_count):
    even, odd = ring_partners(ice_count)
    far = [(a, (a + atm_count // 2) % atm_count) for a in range(atm_count)]
    return [
        pieces[0],
        lax.ppermute(pieces[1], "ice", list(enumerate(even))),
        lax.ppermute(pieces[2], "ice", list(enumerate(odd))),
        lax.ppermute(pieces[3], "atm", far),
    ]


def on_device(driver, records, position, weight, temp, water, density, limit):
    fields, rows = driver.shape
    atm_count = lax.axis_size("atm")
    ice_count = lax.axis_size("ice")
    mesh_shape = (atm_count, ice_count)
    owners = atm_count * ice_count
    slots = records.shape[0] // owners
    records = records.reshape(owners, slots // LANES, LANES)
    *picked, index = pick_rows(mesh_shape, records, driver)
    tables = swap_partners(picked, atm_count, ice_count)
    *sums, temp_new, water_new = cell_sums(
        mesh_shape, lay_flat(position), lay_flat(weight), temp, water, density, limit, tables
    )
    returned = swap_partners(sums, atm_count, ice_count)
    balance, albedo = row_sums(index, returned, rows)
    return balance.reshape(rows), albedo.reshape(rows), temp_new, water_new


def solution(mesh):
    both = ("atm", "ice")
    return jax.shard_map(
        on_device,
        mesh=mesh,
        in_specs=(P(None, both), P(both)) + (P(None, both),) * 6,
        out_specs=(P(both), P(both), P(None, both), P(None, both)),
        check_vma=False,
    )
```

profile of v0, /device:TPU:0, one launch (start us, length us, event | category | flops | bytes accessed | tf_op | source)
XLA Modules:
  0.0 50.4 jit_solution(2931100566770166611)
XLA Ops:
  0.6 3.1 %pick_rows.1 = (f32[8,512]{1,0:T(8,128)}, f32[8,512]{1,0:T(8,128)}, f32[8,512]{1,0:T(8,128)}, f32[8,512]{1,0:T(8,128)}, s32[16,128]{1,0:T(8,128)}) custom-call(s32[128,4,128]{2,1,0:T(4,128)} %bitcast.15, f32[8,10240]{1,0:T(8,128)} %driver_any.1), custom_call_target="tpu_custom_call" | custom-call | tf_op jit(solution)/shard_map/pick_rows/pallas_call | solution.py:78
  3.7 2.1 %collective-permute-start = (f32[8,512]{1,0:T(8,128)}, f32[8,512]{1,0:T(8,128)S(1)}, u32[]{:S(2)}, u32[]{:S(2)}) collective-permute-start(f32[8,512]{1,0:T(8,128)} %get-tuple-element.19), channel_id=1, source_target_pairs={{0,1},{1,0},{2,3},{3,2},{4,5},{5,4},{6,7},{7,6},{8,9},{9,8},{10,11... | collective-permute-start | bytes 49160 | tf_op jit(solution)/shard_map/ppermute | solution.py:505
  5.8 5.0 %collective-permute-start.1 = (f32[8,512]{1,0:T(8,128)}, f32[8,512]{1,0:T(8,128)S(1)}, u32[]{:S(2)}, u32[]{:S(2)}) collective-permute-start(f32[8,512]{1,0:T(8,128)} %get-tuple-element.20), channel_id=1, source_target_pairs={{0,15},{1,2},{2,1},{3,4},{4,3},{5,6},{6,5},{7,8},{8,7},{9,10},{10,... | collective-permute-start | bytes 49160 | tf_op jit(solution)/shard_map/ppermute | solution.py:506
  10.8 3.0 %collective-permute-start.2 = (f32[8,512]{1,0:T(8,128)}, f32[8,512]{1,0:T(8,128)S(1)}, u32[]{:S(2)}, u32[]{:S(2)}) collective-permute-start(f32[8,512]{1,0:T(8,128)} %get-tuple-element.21), channel_id=1, source_target_pairs={{0,64},{16,80},{32,96},{48,112},{64,0},{80,16},{96,32},{112,48},{1... | collective-permute-start | bytes 49160 | tf_op jit(solution)/shard_map/ppermute | solution.py:507
  13.8 0.0 collective-permute-done.refs_7_
  13.8 0.0 copy-start.2
  13.8 0.0 collective-permute-done.1.refs_8_
  13.8 0.0 copy-start.3
  13.8 2.4 %collective-permute-done.2.refs_9_ = f32[8,512]{1,0:T(8,128)S(1)} collective-permute-done((f32[8,512]{1,0:T(8,128)}, f32[8,512]{1,0:T(8,128)S(1)}, u32[]{:S(2)}, u32[]{:S(2)}) %collective-permute-start.2) | collective-permute-done | bytes 16416 | tf_op jit(solution)/shard_map/ppermute | solution.py:507
  16.2 0.0 copy-start.4
  16.2 0.0 copy-done.2
  16.2 0.0 copy-done.3
  16.2 0.6 %copy-done.4 = f32[8,512]{1,0:T(8,128)} copy-done((f32[8,512]{1,0:T(8,128)}, f32[8,512]{1,0:T(8,128)S(1)}, u32[]{:S(2)}) %copy-start.4) | copy-done | bytes 16408
  16.8 0.0 copy-start
  16.8 24.4 %cell_sums.1 = (f32[2,512]{1,0:T(2,128)}, f32[2,512]{1,0:T(2,128)}, f32[2,512]{1,0:T(2,128)}, f32[2,512]{1,0:T(2,128)}, f32[30,16384]{1,0:T(8,128)}, /*index=5*/f32[30,16384]{1,0:T(8,128)}) custom-call(s32[512,128]{1,0:T(8,128)} %bitcast.13, f32[512,128]{1,0:T(8,128)} %bitcast.14, f32[30,16384]{1,0:T(8,128)} %refs_2_.1, f32[30,16384]{1,0:T(8,128)} %refs_3_.1, ...), custom_call_target="tpu_custom_call" | custom-call | tf_op jit(solution)/shard_map/cell_sums/pallas_call | solution.py:422
  41.2 0.1 collective-permute-start.3
  41.3 1.9 %collective-permute-start.4 = (f32[2,512]{1,0:T(2,128)}, f32[2,512]{1,0:T(2,128)S(1)}, u32[]{:S(2)}, u32[]{:S(2)}) collective-permute-start(f32[2,512]{1,0:T(2,128)} %get-tuple-element.24), channel_id=1, source_target_pairs={{0,15},{1,2},{2,1},{3,4},{4,3},{5,6},{6,5},{7,8},{8,7},{9,10},{10,... | collective-permute-start | bytes 12296 | tf_op jit(solution)/shard_map/ppermute | solution.py:506
  43.3 3.0 %collective-permute-start.5 = (f32[2,512]{1,0:T(2,128)}, f32[2,512]{1,0:T(2,128)S(1)}, u32[]{:S(2)}, u32[]{:S(2)}) collective-permute-start(f32[2,512]{1,0:T(2,128)} %get-tuple-element.25), channel_id=1, source_target_pairs={{0,64},{16,80},{32,96},{48,112},{64,0},{80,16},{96,32},{112,48},{1... | collective-permute-start | bytes 12296 | tf_op jit(solution)/shard_map/ppermute | solution.py:507
  46.3 0.0 collective-permute-done.3.p1
  46.3 2.2 %collective-permute-done.4.p2 = f32[2,512]{1,0:T(2,128)S(1)} collective-permute-done((f32[2,512]{1,0:T(2,128)}, f32[2,512]{1,0:T(2,128)S(1)}, u32[]{:S(2)}, u32[]{:S(2)}) %collective-permute-start.4) | collective-permute-done | bytes 4128 | tf_op jit(solution)/shard_map/ppermute | solution.py:506
  48.6 0.0 collective-permute-done.5.p3
  48.6 0.0 copy-done
  48.6 0.0 copy-start.1
  48.6 0.7 %copy-done.1 = f32[2,512]{1,0:T(2,128)S(1)} copy-done((f32[2,512]{1,0:T(2,128)S(1)}, f32[2,512]{1,0:T(2,128)}, u32[]{:S(2)}) %copy-start.1) | copy-done | bytes 4120
  49.3 1.1 %row_sums.1 = (f32[80,128]{1,0:T(8,128)}, f32[80,128]{1,0:T(8,128)}) custom-call(s32[16,128]{1,0:T(8,128)S(1)} %copy-done, f32[2,512]{1,0:T(2,128)S(1)} %copy-done.1, f32[2,512]{1,0:T(2,128)S(1)} %collective-permute-done.3.p1, f32[2,512]{1,0:T(2,128)S(1)} %collective-permute-done.4.p2, f32[2,512]{1,0:T(2,128)S(1)} %collective-permute-done.5.p3), custom_call_target="tpu_custom_call" | custom-call | tf_op jit(solution)/shard_map/row_sums/pallas_call | solution.py:477
Async XLA Ops:
  3.7 10.1 %collective-permute-start = (f32[8,512]{1,0:T(8,128)}, f32[8,512]{1,0:T(8,128)S(1)}, u32[]{:S(2)}, u32[]{:S(2)}) collective-permute-start(f32[8,512]{1,0:T(8,128)} %get-tuple-element.19), channel_id=1, source_target_pairs={{0,1},{1,0},{2,3},{3,2},{4,5},{5,4},{6,7},{7,6},{8,9},{9,8},{10,11... | collective-permute-start | bytes 49160 | tf_op jit(solution)/shard_map/ppermute | solution.py:505
  5.8 8.0 %collective-permute-start.1 = (f32[8,512]{1,0:T(8,128)}, f32[8,512]{1,0:T(8,128)S(1)}, u32[]{:S(2)}, u32[]{:S(2)}) collective-permute-start(f32[8,512]{1,0:T(8,128)} %get-tuple-element.20), channel_id=1, source_target_pairs={{0,15},{1,2},{2,1},{3,4},{4,3},{5,6},{6,5},{7,8},{8,7},{9,10},{10,... | collective-permute-start | bytes 49160 | tf_op jit(solution)/shard_map/ppermute | solution.py:506
  10.8 5.5 %collective-permute-start.2 = (f32[8,512]{1,0:T(8,128)}, f32[8,512]{1,0:T(8,128)S(1)}, u32[]{:S(2)}, u32[]{:S(2)}) collective-permute-start(f32[8,512]{1,0:T(8,128)} %get-tuple-element.21), channel_id=1, source_target_pairs={{0,64},{16,80},{32,96},{48,112},{64,0},{80,16},{96,32},{112,48},{1... | collective-permute-start | bytes 49160 | tf_op jit(solution)/shard_map/ppermute | solution.py:507
  13.8 2.4 %copy-start.2 = (f32[8,512]{1,0:T(8,128)}, f32[8,512]{1,0:T(8,128)S(1)}, u32[]{:S(2)}) copy-start(f32[8,512]{1,0:T(8,128)S(1)} %collective-permute-done.refs_7_) | copy-start | bytes 49156
  13.8 2.4 %copy-start.3 = (f32[8,512]{1,0:T(8,128)}, f32[8,512]{1,0:T(8,128)S(1)}, u32[]{:S(2)}) copy-start(f32[8,512]{1,0:T(8,128)S(1)} %collective-permute-done.1.refs_8_) | copy-start | bytes 49156
  16.2 0.6 %copy-start.4 = (f32[8,512]{1,0:T(8,128)}, f32[8,512]{1,0:T(8,128)S(1)}, u32[]{:S(2)}) copy-start(f32[8,512]{1,0:T(8,128)S(1)} %collective-permute-done.2.refs_9_) | copy-start | bytes 49156
  16.8 31.8 %copy-start = (s32[16,128]{1,0:T(8,128)S(1)}, s32[16,128]{1,0:T(8,128)}, u32[]{:S(2)}) copy-start(s32[16,128]{1,0:T(8,128)} %get-tuple-element.17.index) | copy-start | bytes 24580
  41.2 5.1 %collective-permute-start.3 = (f32[2,512]{1,0:T(2,128)}, f32[2,512]{1,0:T(2,128)S(1)}, u32[]{:S(2)}, u32[]{:S(2)}) collective-permute-start(f32[2,512]{1,0:T(2,128)} %get-tuple-element.23), channel_id=1, source_target_pairs={{0,1},{1,0},{2,3},{3,2},{4,5},{5,4},{6,7},{7,6},{8,9},{9,8},{10,11... | collective-permute-start | bytes 12296 | tf_op jit(solution)/shard_map/ppermute | solution.py:505
  41.3 7.2 %collective-permute-start.4 = (f32[2,512]{1,0:T(2,128)}, f32[2,512]{1,0:T(2,128)S(1)}, u32[]{:S(2)}, u32[]{:S(2)}) collective-permute-start(f32[2,512]{1,0:T(2,128)} %get-tuple-element.24), channel_id=1, source_target_pairs={{0,15},{1,2},{2,1},{3,4},{4,3},{5,6},{6,5},{7,8},{8,7},{9,10},{10,... | collective-permute-start | bytes 12296 | tf_op jit(solution)/shard_map/ppermute | solution.py:506
  43.3 5.3 %collective-permute-start.5 = (f32[2,512]{1,0:T(2,128)}, f32[2,512]{1,0:T(2,128)S(1)}, u32[]{:S(2)}, u32[]{:S(2)}) collective-permute-start(f32[2,512]{1,0:T(2,128)} %get-tuple-element.25), channel_id=1, source_target_pairs={{0,64},{16,80},{32,96},{48,112},{64,0},{80,16},{96,32},{112,48},{1... | collective-permute-start | bytes 12296 | tf_op jit(solution)/shard_map/ppermute | solution.py:507
  48.6 0.7 %copy-start.1 = (f32[2,512]{1,0:T(2,128)S(1)}, f32[2,512]{1,0:T(2,128)}, u32[]{:S(2)}) copy-start(f32[2,512]{1,0:T(2,128)} %get-tuple-element.22.p0) | copy-start | bytes 12292
where the time goes:
time: 50.6 us; the launch traced here: 50.4 us
  Pallas kernels  28.6 us (57%)
  starting transfers between devices  15.1 us (30%)
  waiting for transfers between devices  4.69 us (9%)
  local copies, waits for them, and re-layouts  1.29 us (3%)
  between operations  0.67 us (1%)
    pallas_call x1, Pallas kernels, cell_sums(): pl.pallas_call(functools.partial(cell_kernel, mesh_shape), grid=(cells //...  24.4 us
    ppermute x2, starting transfers between devices, swap_partners(): lax.ppermute(pieces[2], 'ice', list(enumerate(odd)))  6.9 us
    ppermute x2, starting transfers between devices, swap_partners(): lax.ppermute(pieces[3], 'atm', far)  6.07 us
    pallas_call x1, Pallas kernels, pick_rows(): pl.pallas_call(functools.partial(pick_kernel, mesh_shape), out_shape=[jax...  3.1 us
    ppermute x2, waiting for transfers between devices, swap_partners(): lax.ppermute(pieces[3], 'atm', far)  2.44 us
    ppermute x2, waiting for transfers between devices, swap_partners(): lax.ppermute(pieces[2], 'ice', list(enumerate(odd)))  2.24 us
    ppermute x2, starting transfers between devices, swap_partners(): lax.ppermute(pieces[1], 'ice', list(enumerate(even)))  2.17 us
    unnamed x10, local copies, waits for them, and re-layouts  1.29 us
  transfers between devices with their start and end apart: 6, of which 2 were waited for; matrix products, arithmetic and copies ran while one was open for 0% of the time, Pallas kernels for 0%

commit v1 on v0

--- a/solution.py
+++ b/solution.py
@@ -13,6 +13,9 @@
 TILE = 1024
 F32 = jnp.float32
 BF16 = jnp.bfloat16
+WORDS = 5
+FIXED = (1 << 20) - 1
+TILES = 4
 VMEM_SMALL = 8 << 20
 VMEM_LARGE = 62 << 20
 VMEM_MOST = 65280 << 10
@@ -245,14 +248,15 @@
         above = column
 
 
-def together(main, beside, each):
-    going = True
-    for _ in main:
-        for _ in range(each):
-            if going:
-                going = next(beside, False) is None
-    for _ in beside:
-        pass
+def together(*lines):
+    ticks = 64
+    for tick in range(1, ticks + 1):
+        for steps, length in lines:
+            for _ in range(length * tick // ticks - length * (tick - 1) // ticks):
+                next(steps, None)
+    for steps, _ in lines:
+        for _ in steps:
+            pass
 
 
 def two_terms(value):
@@ -260,19 +264,44 @@
     return first, value - first
 
 
-def gather_steps(table, low, high, weights, fields, chunks, forced):
+def make_words(rows, scale):
+    q = (rows * scale + 0.5).astype(jnp.int32)
+    q = [spread(q[f : f + 1, :]) for f in range(8)]
+    return [
+        q[0] | ((q[5] & 0xFFF) << 20),
+        q[1] | ((q[5] >> 12) << 20) | ((q[6] & 0xF) << 28),
+        q[2] | (((q[6] >> 4) & 0xFFF) << 20),
+        q[3] | ((q[6] >> 16) << 20) | ((q[7] & 0xFF) << 24),
+        q[4] | ((q[7] >> 8) << 20),
+    ]
+
+
+def from_words(words):
+    def high(word, bits):
+        return lax.shift_right_logical(word, jnp.full(word.shape, bits, jnp.int32))
+
+    q = [word & FIXED for word in words]
+    q.append(high(words[0], 20) | ((high(words[1], 20) & 0xFF) << 12))
+    q.append(
+        high(words[1], 28) | (high(words[2], 20) << 4) | ((high(words[3], 20) & 0xF) << 16)
+    )
+    q.append(high(words[3], 24) | (high(words[4], 20) << 8))
+    return [value.astype(F32) for value in q]
+
+
+def gather_steps(table, low, high, weights, chunks, forced):
     for k in range(len(low)):
-        found = [jnp.zeros((8, LANES), F32) for _ in range(fields)]
+        found = [jnp.zeros((8, LANES), jnp.int32) for _ in range(WORDS)]
         for c in range(chunks):
             here = high[k] == c
-            for f in range(fields):
+            for n in range(WORDS):
                 value = jnp.take_along_axis(
-                    table[pl.ds((c * fields + f) * 8, 8), :], low[k], axis=1
+                    table[pl.ds((c * WORDS + n) * 8, 8), :], low[k], axis=1
                 )
-                found[f] = jnp.where(here, value, found[f])
+                found[n] = jnp.where(here, value, found[n])
             yield
-        for f in range(fields):
-            part = found[f] * weights[k]
+        for f, value in enumerate(from_words(found)):
+            part = value * weights[k]
             forced[f] = part if k == 0 else forced[f] + part
 
 
@@ -320,7 +349,8 @@
 def cell_kernel(mesh_shape, *refs):
     position, weight, temp, water, density, limit, t0, t1, t2, t3 = refs[:10]
     o0, o1, o2, o3, temp_out, water_out = refs[10:16]
-    table, total, st, sw, sd, sl, ot, ow = refs[16:]
+    table, units, total = refs[16:19]
+    laid = (refs[19:25], refs[25:31])
     fields, slots = t0.shape
     per_place = slots // LANES
     chunks = 4 * per_place
@@ -329,18 +359,28 @@
 
     @pl.when(pl.program_id(0) == 0)
     def _():
+        rows = [
+            (t0, t1, t2, t3)[c // per_place][
+                :, (c % per_place) * LANES : (c % per_place + 1) * LANES
+            ]
+            for c in range(chunks)
+        ]
+        most = rows[0]
+        for row in rows[1:]:
+            most = jnp.maximum(most, row)
+        most = jnp.broadcast_to(jnp.max(most, axis=1, keepdims=True), (fields, LANES))
+        most = jnp.maximum(most, 1e-30)
+        scale = float(FIXED) / most
+        for f in range(fields):
+            units[pl.ds(f * 8, 8), :] = spread(most[f : f + 1, :] * (1.0 / FIXED))
         for c in range(chunks):
-            piece = (t0, t1, t2, t3)[c // per_place]
-            j = c % per_place
-            for f in range(fields):
-                table[pl.ds((c * fields + f) * 8, 8), :] = spread(
-                    piece[f : f + 1, j * LANES : (j + 1) * LANES]
-                )
+            for n, word in enumerate(make_words(rows[c], scale)):
+                table[pl.ds((c * WORDS + n) * 8, 8), :] = word
         total[...] = jnp.zeros(total.shape, F32)
 
-    @pl.loop(0, width // TILE)
-    def _(tile):
-        column = pl.multiple_of(tile * TILE, TILE)
+    def load(tile):
+        st, sw, sd, sl, ot, ow = laid[tile % 2]
+        column = tile * TILE
         low = []
         high = []
         weights = []
@@ -358,17 +398,19 @@
         to_layers(density, sd, column, layers)
         to_layers(water, sw, column, layers)
         to_layers(limit, sl, column, layers)
-        forced = [None] * fields
-        firn = {}
-        together(
-            gather_steps(table, low, high, weights, fields, chunks, forced),
-            deep_steps(st, sw, sd, sl, ot, ow, layers, firn),
-            4,
-        )
+        state = {"low": low, "high": high, "weights": weights, "forced": [None] * fields}
+        first = [
+            (gather_steps(table, low, high, weights, chunks, state["forced"]), 64),
+            (deep_steps(*laid[tile % 2], layers, state), 230),
+        ]
+        return state, first
+
+    def surface(tile, state):
+        forced = [value * units[pl.ds(f * 8, 8), :] for f, value in enumerate(state["forced"])]
         air = 2.0 * forced[0] - 1.0
         short, long, snow, rain, humid, wind, press = forced[1:]
         albedo = 0.45 + 0.4 * snow / (snow + 0.1) - 0.1 * jnp.maximum(air, 0.0)
-        skin = layer(st, 0)
+        skin = layer(laid[tile % 2][0], 0)
         flux = (
             1.5 * (1.0 - albedo) * short
             + 0.6 * (long - 0.5)
@@ -376,24 +418,37 @@
             + 0.3 * wind * (humid - press)
         )
         top = skin + 0.5 * flux
-        balance = snow + rain - firn["runoff"] - 0.2 * wind * (press - humid)
-        together(
-            scatter_steps(total, low, high, weights, (balance, albedo), chunks),
-            upper_steps(
-                st,
-                sw,
-                sd,
-                sl,
-                ot,
-                ow,
-                jnp.minimum(top, 0.0),
-                jnp.maximum(top, 0.0) + rain,
-                firn["columns"],
+        balance = snow + rain - state["runoff"] - 0.2 * wind * (press - humid)
+        return [
+            (
+                scatter_steps(
+                    total, state["low"], state["high"], state["weights"], (balance, albedo), chunks
+                ),
+                32,
             ),
-            3,
-        )
-        from_layers(temp_out, ot, column, layers)
-        from_layers(water_out, ow, column, layers)
+            (
+                upper_steps(
+                    *laid[tile % 2],
+                    jnp.minimum(top, 0.0),
+                    jnp.maximum(top, 0.0) + rain,
+                    state["columns"],
+                ),
+                54,
+            ),
+        ]
+
+    tiles = width // TILE
+    state, first = load(0)
+    together(*first)
+    for tile in range(tiles):
+        lines = surface(tile, state)
+        if tile + 1 < tiles:
+            state, first = load(tile + 1)
+            lines += first
+        together(*lines)
+        ot, ow = laid[tile % 2][4:]
+        from_layers(temp_out, ot, tile * TILE, layers)
+        from_layers(water_out, ow, tile * TILE, layers)
 
     @pl.when(pl.program_id(0) == pl.num_programs(0) - 1)
     def _():
@@ -413,7 +468,7 @@
     fields, slots = tables[0].shape
     chunks = 4 * slots // LANES
     layers, cells = temp.shape
-    width = min(cells, 2 * TILE)
+    width = min(cells, TILES * TILE)
     firn = pl.BlockSpec((layers, width), lambda g: (0, g))
     flat = pl.BlockSpec((4 * width // LANES, LANES), lambda g: (g, 0))
     table = pl.BlockSpec((fields, slots), lambda g: (0, 0))
@@ -427,10 +482,11 @@
         in_specs=[flat] * 2 + [firn] * 4 + [table] * 4,
         out_specs=[sums] * 4 + [firn] * 2,
         scratch_shapes=[
-            pltpu.VMEM((chunks * fields * 8, LANES), F32),
+            pltpu.VMEM((chunks * WORDS * 8, LANES), jnp.int32),
+            pltpu.VMEM((fields * 8, LANES), F32),
             pltpu.VMEM((LANES, 4 * chunks), F32),
         ]
-        + [pltpu.VMEM((padded, LANES), F32)] * 6,
+        + [pltpu.VMEM((padded, LANES), F32)] * 12,
         compiler_params=kernel_params(VMEM_LARGE),
         name="cell_sums",
     )(position, weight, temp, water, density, limit, *tables)

time: 50.6 us -> 43.2 us (0.85)
  Pallas kernels: 28.6 us -> 21.2 us
    pallas_call x1, Pallas kernels: 24.4 us -> 17 us  [cell_sums(): pl.pallas_call(functools.partial(cell_kernel, mesh_shape), grid=(cells //...]
where the time goes in v1:
time: 43.2 us; the launch traced here: 43 us
  Pallas kernels  21.2 us (49%)
  starting transfers between devices  15.1 us (35%)
  waiting for transfers between devices  4.73 us (11%)
  local copies, waits for them, and re-layouts  1.29 us (3%)
  between operations  0.67 us (2%)
    pallas_call x1, Pallas kernels, cell_sums(): pl.pallas_call(functools.partial(cell_kernel, mesh_shape), grid=(cells //...  17 us
    ppermute x2, starting transfers between devices, swap_partners(): lax.ppermute(pieces[2], 'ice', list(enumerate(odd)))  6.91 us
    ppermute x2, starting transfers between devices, swap_partners(): lax.ppermute(pieces[3], 'atm', far)  6.03 us
    pallas_call x1, Pallas kernels, pick_rows(): pl.pallas_call(functools.partial(pick_kernel, mesh_shape), out_shape=[jax...  3.1 us
    ppermute x2, waiting for transfers between devices, swap_partners(): lax.ppermute(pieces[3], 'atm', far)  2.45 us
    ppermute x2, waiting for transfers between devices, swap_partners(): lax.ppermute(pieces[2], 'ice', list(enumerate(odd)))  2.28 us
    ppermute x2, starting transfers between devices, swap_partners(): lax.ppermute(pieces[1], 'ice', list(enumerate(even)))  2.17 us
    unnamed x10, local copies, waits for them, and re-layouts  1.29 us
  transfers between devices with their start and end apart: 6, of which 2 were waited for; matrix products, arithmetic and copies ran while one was open for 0% of the time, Pallas kernels for 0%

profile of v1, /device:TPU:0, one launch (start us, length us, event | category | flops | bytes accessed | tf_op | source)
XLA Modules:
  0.0 43.0 jit_solution(17150864933603346909)
XLA Ops:
  0.6 3.1 %pick_rows.1 = (f32[8,512]{1,0:T(8,128)}, f32[8,512]{1,0:T(8,128)}, f32[8,512]{1,0:T(8,128)}, f32[8,512]{1,0:T(8,128)}, s32[16,128]{1,0:T(8,128)}) custom-call(s32[128,4,128]{2,1,0:T(4,128)} %bitcast.15, f32[8,10240]{1,0:T(8,128)} %driver_any.1), custom_call_target="tpu_custom_call" | custom-call | tf_op jit(solution)/shard_map/pick_rows/pallas_call | solution.py:81
  3.7 2.1 %collective-permute-start = (f32[8,512]{1,0:T(8,128)}, f32[8,512]{1,0:T(8,128)S(1)}, u32[]{:S(2)}, u32[]{:S(2)}) collective-permute-start(f32[8,512]{1,0:T(8,128)} %get-tuple-element.19), channel_id=1, source_target_pairs={{0,1},{1,0},{2,3},{3,2},{4,5},{5,4},{6,7},{7,6},{8,9},{9,8},{10,11... | collective-permute-start | bytes 49160 | tf_op jit(solution)/shard_map/ppermute | solution.py:561
  5.8 5.0 %collective-permute-start.1 = (f32[8,512]{1,0:T(8,128)}, f32[8,512]{1,0:T(8,128)S(1)}, u32[]{:S(2)}, u32[]{:S(2)}) collective-permute-start(f32[8,512]{1,0:T(8,128)} %get-tuple-element.20), channel_id=1, source_target_pairs={{0,15},{1,2},{2,1},{3,4},{4,3},{5,6},{6,5},{7,8},{8,7},{9,10},{10,... | collective-permute-start | bytes 49160 | tf_op jit(solution)/shard_map/ppermute | solution.py:562
  10.8 3.0 %collective-permute-start.2 = (f32[8,512]{1,0:T(8,128)}, f32[8,512]{1,0:T(8,128)S(1)}, u32[]{:S(2)}, u32[]{:S(2)}) collective-permute-start(f32[8,512]{1,0:T(8,128)} %get-tuple-element.21), channel_id=1, source_target_pairs={{0,64},{16,80},{32,96},{48,112},{64,0},{80,16},{96,32},{112,48},{1... | collective-permute-start | bytes 49160 | tf_op jit(solution)/shard_map/ppermute | solution.py:563
  13.8 0.0 collective-permute-done.refs_7_
  13.8 0.0 copy-start.2
  13.8 0.0 collective-permute-done.1.refs_8_
  13.8 0.0 copy-start.3
  13.8 2.4 %collective-permute-done.2.refs_9_ = f32[8,512]{1,0:T(8,128)S(1)} collective-permute-done((f32[8,512]{1,0:T(8,128)}, f32[8,512]{1,0:T(8,128)S(1)}, u32[]{:S(2)}, u32[]{:S(2)}) %collective-permute-start.2) | collective-permute-done | bytes 16416 | tf_op jit(solution)/shard_map/ppermute | solution.py:563
  16.2 0.0 copy-start.4
  16.2 0.0 copy-done.2
  16.2 0.0 copy-done.3
  16.2 0.6 %copy-done.4 = f32[8,512]{1,0:T(8,128)} copy-done((f32[8,512]{1,0:T(8,128)}, f32[8,512]{1,0:T(8,128)S(1)}, u32[]{:S(2)}) %copy-start.4) | copy-done | bytes 16408
  16.8 0.0 copy-start
  16.8 17.0 %cell_sums.1 = (f32[2,512]{1,0:T(2,128)}, f32[2,512]{1,0:T(2,128)}, f32[2,512]{1,0:T(2,128)}, f32[2,512]{1,0:T(2,128)}, f32[30,16384]{1,0:T(8,128)}, /*index=5*/f32[30,16384]{1,0:T(8,128)}) custom-call(s32[512,128]{1,0:T(8,128)} %bitcast.13, f32[512,128]{1,0:T(8,128)} %bitcast.14, f32[30,16384]{1,0:T(8,128)} %refs_2_.1, f32[30,16384]{1,0:T(8,128)} %refs_3_.1, ...), custom_call_target="tpu_custom_call" | custom-call | tf_op jit(solution)/shard_map/cell_sums/pallas_call | solution.py:477
  33.8 0.1 collective-permute-start.3
  33.9 1.9 %collective-permute-start.4 = (f32[2,512]{1,0:T(2,128)}, f32[2,512]{1,0:T(2,128)S(1)}, u32[]{:S(2)}, u32[]{:S(2)}) collective-permute-start(f32[2,512]{1,0:T(2,128)} %get-tuple-element.24), channel_id=1, source_target_pairs={{0,15},{1,2},{2,1},{3,4},{4,3},{5,6},{6,5},{7,8},{8,7},{9,10},{10,... | collective-permute-start | bytes 12296 | tf_op jit(solution)/shard_map/ppermute | solution.py:562
  35.9 3.0 %collective-permute-start.5 = (f32[2,512]{1,0:T(2,128)}, f32[2,512]{1,0:T(2,128)S(1)}, u32[]{:S(2)}, u32[]{:S(2)}) collective-permute-start(f32[2,512]{1,0:T(2,128)} %get-tuple-element.25), channel_id=1, source_target_pairs={{0,64},{16,80},{32,96},{48,112},{64,0},{80,16},{96,32},{112,48},{1... | collective-permute-start | bytes 12296 | tf_op jit(solution)/shard_map/ppermute | solution.py:563
  38.9 0.0 collective-permute-done.3.p1
  38.9 2.3 %collective-permute-done.4.p2 = f32[2,512]{1,0:T(2,128)S(1)} collective-permute-done((f32[2,512]{1,0:T(2,128)}, f32[2,512]{1,0:T(2,128)S(1)}, u32[]{:S(2)}, u32[]{:S(2)}) %collective-permute-start.4) | collective-permute-done | bytes 4128 | tf_op jit(solution)/shard_map/ppermute | solution.py:562
  41.2 0.0 collective-permute-done.5.p3
  41.2 0.0 copy-done
  41.2 0.0 copy-start.1
  41.2 0.7 %copy-done.1 = f32[2,512]{1,0:T(2,128)S(1)} copy-done((f32[2,512]{1,0:T(2,128)S(1)}, f32[2,512]{1,0:T(2,128)}, u32[]{:S(2)}) %copy-start.1) | copy-done | bytes 4120
  41.9 1.1 %row_sums.1 = (f32[80,128]{1,0:T(8,128)}, f32[80,128]{1,0:T(8,128)}) custom-call(s32[16,128]{1,0:T(8,128)S(1)} %copy-done, f32[2,512]{1,0:T(2,128)S(1)} %copy-done.1, f32[2,512]{1,0:T(2,128)S(1)} %collective-permute-done.3.p1, f32[2,512]{1,0:T(2,128)S(1)} %collective-permute-done.4.p2, f32[2,512]{1,0:T(2,128)S(1)} %collective-permute-done.5.p3), custom_call_target="tpu_custom_call" | custom-call | tf_op jit(solution)/shard_map/row_sums/pallas_call | solution.py:533
Async XLA Ops:
  3.7 10.1 %collective-permute-start = (f32[8,512]{1,0:T(8,128)}, f32[8,512]{1,0:T(8,128)S(1)}, u32[]{:S(2)}, u32[]{:S(2)}) collective-permute-start(f32[8,512]{1,0:T(8,128)} %get-tuple-element.19), channel_id=1, source_target_pairs={{0,1},{1,0},{2,3},{3,2},{4,5},{5,4},{6,7},{7,6},{8,9},{9,8},{10,11... | collective-permute-start | bytes 49160 | tf_op jit(solution)/shard_map/ppermute | solution.py:561
  5.8 8.0 %collective-permute-start.1 = (f32[8,512]{1,0:T(8,128)}, f32[8,512]{1,0:T(8,128)S(1)}, u32[]{:S(2)}, u32[]{:S(2)}) collective-permute-start(f32[8,512]{1,0:T(8,128)} %get-tuple-element.20), channel_id=1, source_target_pairs={{0,15},{1,2},{2,1},{3,4},{4,3},{5,6},{6,5},{7,8},{8,7},{9,10},{10,... | collective-permute-start | bytes 49160 | tf_op jit(solution)/shard_map/ppermute | solution.py:562
  10.8 5.5 %collective-permute-start.2 = (f32[8,512]{1,0:T(8,128)}, f32[8,512]{1,0:T(8,128)S(1)}, u32[]{:S(2)}, u32[]{:S(2)}) collective-permute-start(f32[8,512]{1,0:T(8,128)} %get-tuple-element.21), channel_id=1, source_target_pairs={{0,64},{16,80},{32,96},{48,112},{64,0},{80,16},{96,32},{112,48},{1... | collective-permute-start | bytes 49160 | tf_op jit(solution)/shard_map/ppermute | solution.py:563
  13.8 2.4 %copy-start.2 = (f32[8,512]{1,0:T(8,128)}, f32[8,512]{1,0:T(8,128)S(1)}, u32[]{:S(2)}) copy-start(f32[8,512]{1,0:T(8,128)S(1)} %collective-permute-done.refs_7_) | copy-start | bytes 49156
  13.8 2.4 %copy-start.3 = (f32[8,512]{1,0:T(8,128)}, f32[8,512]{1,0:T(8,128)S(1)}, u32[]{:S(2)}) copy-start(f32[8,512]{1,0:T(8,128)S(1)} %collective-permute-done.1.refs_8_) | copy-start | bytes 49156
  16.2 0.6 %copy-start.4 = (f32[8,512]{1,0:T(8,128)}, f32[8,512]{1,0:T(8,128)S(1)}, u32[]{:S(2)}) copy-start(f32[8,512]{1,0:T(8,128)S(1)} %collective-permute-done.2.refs_9_) | copy-start | bytes 49156
  16.8 24.4 %copy-start = (s32[16,128]{1,0:T(8,128)S(1)}, s32[16,128]{1,0:T(8,128)}, u32[]{:S(2)}) copy-start(s32[16,128]{1,0:T(8,128)} %get-tuple-element.17.index) | copy-start | bytes 24580
  33.8 5.0 %collective-permute-start.3 = (f32[2,512]{1,0:T(2,128)}, f32[2,512]{1,0:T(2,128)S(1)}, u32[]{:S(2)}, u32[]{:S(2)}) collective-permute-start(f32[2,512]{1,0:T(2,128)} %get-tuple-element.23), channel_id=1, source_target_pairs={{0,1},{1,0},{2,3},{3,2},{4,5},{5,4},{6,7},{7,6},{8,9},{9,8},{10,11... | collective-permute-start | bytes 12296 | tf_op jit(solution)/shard_map/ppermute | solution.py:561
  33.9 7.2 %collective-permute-start.4 = (f32[2,512]{1,0:T(2,128)}, f32[2,512]{1,0:T(2,128)S(1)}, u32[]{:S(2)}, u32[]{:S(2)}) collective-permute-start(f32[2,512]{1,0:T(2,128)} %get-tuple-element.24), channel_id=1, source_target_pairs={{0,15},{1,2},{2,1},{3,4},{4,3},{5,6},{6,5},{7,8},{8,7},{9,10},{10,... | collective-permute-start | bytes 12296 | tf_op jit(solution)/shard_map/ppermute | solution.py:562
  35.9 5.3 %collective-permute-start.5 = (f32[2,512]{1,0:T(2,128)}, f32[2,512]{1,0:T(2,128)S(1)}, u32[]{:S(2)}, u32[]{:S(2)}) collective-permute-start(f32[2,512]{1,0:T(2,128)} %get-tuple-element.25), channel_id=1, source_target_pairs={{0,64},{16,80},{32,96},{48,112},{64,0},{80,16},{96,32},{112,48},{1... | collective-permute-start | bytes 12296 | tf_op jit(solution)/shard_map/ppermute | solution.py:563
  41.2 0.7 %copy-start.1 = (f32[2,512]{1,0:T(2,128)S(1)}, f32[2,512]{1,0:T(2,128)}, u32[]{:S(2)}) copy-start(f32[2,512]{1,0:T(2,128)} %get-tuple-element.22.p0) | copy-start | bytes 12292

commit v2 on v1

--- a/solution.py
+++ b/solution.py
@@ -15,10 +15,8 @@
 BF16 = jnp.bfloat16
 WORDS = 5
 FIXED = (1 << 20) - 1
-TILES = 4
-VMEM_SMALL = 8 << 20
-VMEM_LARGE = 62 << 20
-VMEM_MOST = 65280 << 10
+VMEM_SMALL = 6 << 20
+VMEM_MOST = 54950 << 10
 
 
 def kernel_params(limit):
@@ -161,8 +159,8 @@
 
 
 class Column:
-    def __init__(self, temp, water, limit):
-        self.half = -0.5 * temp
+    def __init__(self, temp, water, limit, half=None):
+        self.half = -0.5 * temp if half is None else half
         self.water = water
         self.limit = limit
         self.leaving = {}
@@ -179,6 +177,10 @@
         frozen = jnp.minimum(held, jnp.maximum(self.half, 0.0))
         self.water = held - frozen
         self.half = self.half - 0.75 * frozen
+
+
+def open_layers():
+    return range(DIFFUSION_ITERS + 1, DIFFUSION_ITERS + PERCOLATE_ROUNDS)
 
 
 def deep_steps(st, sw, sd, sl, ot, ow, layers, found):
@@ -346,41 +348,79 @@
         )
 
 
+def tile_groups(tiles):
+    return (0, 1, 5, tiles)
+
+
 def cell_kernel(mesh_shape, *refs):
-    position, weight, temp, water, density, limit, t0, t1, t2, t3 = refs[:10]
-    o0, o1, o2, o3, temp_out, water_out = refs[10:16]
+    afar = refs[:6]
+    t0, t1, t2, t3 = refs[6:10]
+    o0, o1, o2, o3 = refs[10:14]
     table, units, total = refs[16:19]
     laid = (refs[19:25], refs[25:31])
+    near = refs[31:37]
+    position, weight, temp, water, density, limit = near
+    results = refs[37:39]
+    temp_out, water_out = results
+    in_sems, out_sems = refs[39:41]
+    tiles = temp.shape[1] // TILE
+    bounds = tile_groups(tiles)
+    groups = len(bounds) - 1
+
+    def arrivals(group):
+        tile, count = bounds[group], bounds[group + 1] - bounds[group]
+        copies = []
+        for n in range(6):
+            if n < 2:
+                part = (pl.ds(pl.multiple_of(tile * 32, 32), count * 32), slice(None))
+            else:
+                part = (slice(None), pl.ds(pl.multiple_of(tile * TILE, TILE), count * TILE))
+            copies.append(
+                pltpu.make_async_copy(afar[n].at[part], near[n].at[part], in_sems.at[group, n])
+            )
+        return copies
+
+    def departures(group):
+        part = (slice(None), pl.ds(pl.multiple_of(group * 2 * TILE, TILE), 2 * TILE))
+        return [
+            pltpu.make_async_copy(results[n].at[part], refs[14 + n].at[part], out_sems.at[group, n])
+            for n in range(2)
+        ]
+
+    for group in range(groups):
+        for copy in arrivals(group):
+            copy.start()
     fields, slots = t0.shape
     per_place = slots // LANES
     chunks = 4 * per_place
     layers, width = temp.shape
     ids = partner_ids(*mesh_shape)
 
-    @pl.when(pl.program_id(0) == 0)
-    def _():
-        rows = [
-            (t0, t1, t2, t3)[c // per_place][
-                :, (c % per_place) * LANES : (c % per_place + 1) * LANES
-            ]
-            for c in range(chunks)
+    rows = [
+        (t0, t1, t2, t3)[c // per_place][
+            :, (c % per_place) * LANES : (c % per_place + 1) * LANES
         ]
-        most = rows[0]
-        for row in rows[1:]:
-            most = jnp.maximum(most, row)
-        most = jnp.broadcast_to(jnp.max(most, axis=1, keepdims=True), (fields, LANES))
-        most = jnp.maximum(most, 1e-30)
-        scale = float(FIXED) / most
-        for f in range(fields):
-            units[pl.ds(f * 8, 8), :] = spread(most[f : f + 1, :] * (1.0 / FIXED))
-        for c in range(chunks):
-            for n, word in enumerate(make_words(rows[c], scale)):
-                table[pl.ds((c * WORDS + n) * 8, 8), :] = word
-        total[...] = jnp.zeros(total.shape, F32)
-
-    def load(tile):
-        st, sw, sd, sl, ot, ow = laid[tile % 2]
-        column = tile * TILE
+        for c in range(chunks)
+    ]
+    most = rows[0]
+    for row in rows[1:]:
+        most = jnp.maximum(most, row)
+    most = jnp.broadcast_to(jnp.max(most, axis=1, keepdims=True), (fields, LANES))
+    most = jnp.maximum(most, 1e-30)
+    scale = float(FIXED) / most
+    for f in range(fields):
+        units[pl.ds(f * 8, 8), :] = spread(most[f : f + 1, :] * (1.0 / FIXED))
+    for c in range(chunks):
+        for n, word in enumerate(make_words(rows[c], scale)):
+            table[pl.ds((c * WORDS + n) * 8, 8), :] = word
+    total[...] = jnp.zeros(total.shape, F32)
+
+    def columns_of(tile):
+        return pl.multiple_of(tile * TILE, TILE)
+
+    def lines_before(tile, parity, state):
+        st, sw, sd, sl, ot, ow = laid[parity]
+        column = columns_of(tile)
         low = []
         high = []
         weights = []
@@ -398,19 +438,18 @@
         to_layers(density, sd, column, layers)
         to_layers(water, sw, column, layers)
         to_layers(limit, sl, column, layers)
-        state = {"low": low, "high": high, "weights": weights, "forced": [None] * fields}
-        first = [
+        state.update(low=low, high=high, weights=weights, forced=[None] * fields)
+        return [
             (gather_steps(table, low, high, weights, chunks, state["forced"]), 64),
-            (deep_steps(*laid[tile % 2], layers, state), 230),
+            (deep_steps(*laid[parity], layers, state), 230),
         ]
-        return state, first
-
-    def surface(tile, state):
+
+    def surface(parity, state):
         forced = [value * units[pl.ds(f * 8, 8), :] for f, value in enumerate(state["forced"])]
         air = 2.0 * forced[0] - 1.0
         short, long, snow, rain, humid, wind, press = forced[1:]
         albedo = 0.45 + 0.4 * snow / (snow + 0.1) - 0.1 * jnp.maximum(air, 0.0)
-        skin = layer(laid[tile % 2][0], 0)
+        skin = layer(laid[parity][0], 0)
         flux = (
             1.5 * (1.0 - albedo) * short
             + 0.6 * (long - 0.5)
@@ -419,75 +458,97 @@
         )
         top = skin + 0.5 * flux
         balance = snow + rain - state["runoff"] - 0.2 * wind * (press - humid)
+        parts = [balance, albedo, jnp.minimum(top, 0.0), jnp.maximum(top, 0.0) + rain]
+        for m in open_layers():
+            parts += [state["columns"][m].half, state["columns"][m].water]
+        return tuple(parts + state["low"] + state["high"] + state["weights"])
+
+    def lines_after(parity, carry):
+        st, sw, sd, sl, ot, ow = laid[parity]
+        balance, albedo, top, gain = carry[:4]
+        columns = {}
+        for n, m in enumerate(open_layers()):
+            columns[m] = Column(None, carry[5 + 2 * n], layer(sl, m), carry[4 + 2 * n])
+        low, high, weights = carry[-12:-8], carry[-8:-4], carry[-4:]
         return [
-            (
-                scatter_steps(
-                    total, state["low"], state["high"], state["weights"], (balance, albedo), chunks
-                ),
-                32,
-            ),
-            (
-                upper_steps(
-                    *laid[tile % 2],
-                    jnp.minimum(top, 0.0),
-                    jnp.maximum(top, 0.0) + rain,
-                    state["columns"],
-                ),
-                54,
-            ),
+            (scatter_steps(total, low, high, weights, (balance, albedo), chunks), 32),
+            (upper_steps(*laid[parity], top, gain, columns), 54),
         ]
 
-    tiles = width // TILE
-    state, first = load(0)
-    together(*first)
-    for tile in range(tiles):
-        lines = surface(tile, state)
-        if tile + 1 < tiles:
-            state, first = load(tile + 1)
-            lines += first
+    def write(tile, parity):
+        from_layers(temp_out, laid[parity][4], columns_of(tile), layers)
+        from_layers(water_out, laid[parity][5], columns_of(tile), layers)
+
+    def advance(tile, parity, carry):
+        state = {}
+        lines = lines_after(parity, carry) + lines_before(tile + 1, 1 - parity, state)
         together(*lines)
-        ot, ow = laid[tile % 2][4:]
-        from_layers(temp_out, ot, tile * TILE, layers)
-        from_layers(water_out, ow, tile * TILE, layers)
-
-    @pl.when(pl.program_id(0) == pl.num_programs(0) - 1)
-    def _():
-        sums = total[...].T
-        for q in range(2):
-            first = sums[2 * q * chunks : (2 * q + 1) * chunks]
-            second = sums[(2 * q + 1) * chunks : (2 * q + 2) * chunks]
-            both = first + second
-            for c in range(chunks):
-                j = c % per_place
-                (o0, o1, o2, o3)[c // per_place][q : q + 1, j * LANES : (j + 1) * LANES] = both[
-                    c : c + 1, :
-                ]
+        write(tile, parity)
+        return surface(1 - parity, state)
+
+    for copy in arrivals(0):
+        copy.wait()
+    state = {}
+    together(*lines_before(0, 0, state))
+    carry = surface(0, state)
+    def two_tiles(i, carry):
+        carry = advance(2 * i, 0, carry)
+        carry = advance(2 * i + 1, 1, carry)
+        for copy in departures(i):
+            copy.start()
+        return carry
+
+    for group in range(1, groups):
+        for copy in arrivals(group):
+            copy.wait()
+        first, last = bounds[group] // 2, (bounds[group + 1] - 1) // 2
+        carry = lax.fori_loop(first, last, two_tiles, carry)
+    carry = advance(tiles - 2, 0, carry)
+    together(*lines_after(1, carry))
+    write(tiles - 1, 1)
+    for copy in departures(tiles // 2 - 1):
+        copy.start()
+
+    sums = total[...].T
+    for q in range(2):
+        first = sums[2 * q * chunks : (2 * q + 1) * chunks]
+        second = sums[(2 * q + 1) * chunks : (2 * q + 2) * chunks]
+        both = first + second
+        for c in range(chunks):
+            j = c % per_place
+            (o0, o1, o2, o3)[c // per_place][q : q + 1, j * LANES : (j + 1) * LANES] = both[
+                c : c + 1, :
+            ]
+
+    for group in range(tiles // 2):
+        for copy in departures(group):
+            copy.wait()
 
 
 def cell_sums(mesh_shape, position, weight, temp, water, density, limit, tables):
     fields, slots = tables[0].shape
     chunks = 4 * slots // LANES
     layers, cells = temp.shape
-    width = min(cells, TILES * TILE)
-    firn = pl.BlockSpec((layers, width), lambda g: (0, g))
-    flat = pl.BlockSpec((4 * width // LANES, LANES), lambda g: (g, 0))
-    table = pl.BlockSpec((fields, slots), lambda g: (0, 0))
-    sums = pl.BlockSpec((2, slots), lambda g: (0, 0))
+    vmem = pl.BlockSpec(memory_space=pltpu.VMEM)
+    anywhere = pl.BlockSpec(memory_space=pl.ANY)
+    tiles = cells // TILE
     padded = -(-layers // 8) * 64
     return pl.pallas_call(
         functools.partial(cell_kernel, mesh_shape),
-        grid=(cells // width,),
         out_shape=[jax.ShapeDtypeStruct((2, slots), F32)] * 4
         + [jax.ShapeDtypeStruct((layers, cells), F32)] * 2,
-        in_specs=[flat] * 2 + [firn] * 4 + [table] * 4,
-        out_specs=[sums] * 4 + [firn] * 2,
+        in_specs=[anywhere] * 6 + [vmem] * 4,
+        out_specs=[vmem] * 4 + [anywhere] * 2,
         scratch_shapes=[
             pltpu.VMEM((chunks * WORDS * 8, LANES), jnp.int32),
             pltpu.VMEM((fields * 8, LANES), F32),
             pltpu.VMEM((LANES, 4 * chunks), F32),
         ]
-        + [pltpu.VMEM((padded, LANES), F32)] * 12,
-        compiler_params=kernel_params(VMEM_LARGE),
+        + [pltpu.VMEM((padded, LANES), F32)] * 12
+        + [pltpu.VMEM(position.shape, jnp.int32), pltpu.VMEM(weight.shape, F32)]
+        + [pltpu.VMEM((layers, cells), F32)] * 6
+        + [pltpu.SemaphoreType.DMA((3, 6)), pltpu.SemaphoreType.DMA((tiles // 2, 2))],
+        compiler_params=kernel_params(VMEM_MOST),
         name="cell_sums",
     )(position, weight, temp, water, density, limit, *tables)
 

time: 43.2 us -> 39.2 us (0.907)
  Pallas kernels: 21.2 us -> 19 us
  local copies, waits for them, and re-layouts: 1.29 us -> 0 us
    pallas_call x1, Pallas kernels: 17 us -> 15.3 us  [cell_sums(): pl.pallas_call(functools.partial(cell_kernel, mesh_shape), out_shape=[jax...]
    unnamed x10 -> x0, local copies, waits for them, and re-layouts: 1.29 us -> none
    pallas_call x1, Pallas kernels: 3.1 us -> 2.49 us  [pick_rows(): pl.pallas_call(functools.partial(pick_kernel, mesh_shape), out_shape=[jax...]
where the time goes in v2:
time: 39.2 us; the launch traced here: 39 us
  Pallas kernels  19 us (48%)
  starting transfers between devices  15.1 us (39%)
  waiting for transfers between devices  4.31 us (11%)
  between operations  0.66 us (2%)
    pallas_call x1, Pallas kernels, cell_sums(): pl.pallas_call(functools.partial(cell_kernel, mesh_shape), out_shape=[jax...  15.3 us
    ppermute x2, starting transfers between devices, swap_partners(): lax.ppermute(pieces[2], 'ice', list(enumerate(odd)))  6.89 us
    ppermute x2, starting transfers between devices, swap_partners(): lax.ppermute(pieces[3], 'atm', far)  6.04 us
    pallas_call x1, Pallas kernels, pick_rows(): pl.pallas_call(functools.partial(pick_kernel, mesh_shape), out_shape=[jax...  2.49 us
    ppermute x2, waiting for transfers between devices, swap_partners(): lax.ppermute(pieces[3], 'atm', far)  2.23 us
    ppermute x2, starting transfers between devices, swap_partners(): lax.ppermute(pieces[1], 'ice', list(enumerate(even)))  2.17 us
    ppermute x2, waiting for transfers between devices, swap_partners(): lax.ppermute(pieces[2], 'ice', list(enumerate(odd)))  2.07 us
    pallas_call x1, Pallas kernels, row_sums(): pl.pallas_call(row_kernel, out_shape=[jax.ShapeDtypeStruct((blocks, LANES...  1.13 us
  transfers between devices with their start and end apart: 6, of which 2 were waited for; matrix products, arithmetic and copies ran while one was open for 0% of the time, Pallas kernels for 0%

profile of v2, /device:TPU:0, one launch (start us, length us, event | category | flops | bytes accessed | tf_op | source)
XLA Modules:
  0.0 39.0 jit_solution(1048998687816210262)
XLA Ops:
  0.6 2.5 %pick_rows.1 = (f32[8,512]{1,0:T(8,128)S(1)}, f32[8,512]{1,0:T(8,128)S(1)}, f32[8,512]{1,0:T(8,128)S(1)}, f32[8,512]{1,0:T(8,128)S(1)}, s32[16,128]{1,0:T(8,128)S(1)}) custom-call(s32[128,4,128]{2,1,0:T(4,128)} %bitcast.15, f32[8,10240]{1,0:T(8,128)} %driver_any.1), custom_call_target="tpu_custom_call" | custom-call | tf_op jit(solution)/shard_map/pick_rows/pallas_call | solution.py:79
  3.1 2.1 %collective-permute-start = (f32[8,512]{1,0:T(8,128)S(1)}, f32[8,512]{1,0:T(8,128)S(1)}, u32[]{:S(2)}, u32[]{:S(2)}) collective-permute-start(f32[8,512]{1,0:T(8,128)S(1)} %get-tuple-element.19), channel_id=1, source_target_pairs={{0,1},{1,0},{2,3},{3,2},{4,5},{5,4},{6,7},{7,6},{8,9},{9,8},{10,11... | collective-permute-start | bytes 49160 | tf_op jit(solution)/shard_map/ppermute | solution.py:622
  5.2 5.0 %collective-permute-start.1 = (f32[8,512]{1,0:T(8,128)S(1)}, f32[8,512]{1,0:T(8,128)S(1)}, u32[]{:S(2)}, u32[]{:S(2)}) collective-permute-start(f32[8,512]{1,0:T(8,128)S(1)} %get-tuple-element.20), channel_id=1, source_target_pairs={{0,15},{1,2},{2,1},{3,4},{4,3},{5,6},{6,5},{7,8},{8,7},{9,10},{10,... | collective-permute-start | bytes 49160 | tf_op jit(solution)/shard_map/ppermute | solution.py:623
  10.2 3.0 %collective-permute-start.2 = (f32[8,512]{1,0:T(8,128)S(1)}, f32[8,512]{1,0:T(8,128)S(1)}, u32[]{:S(2)}, u32[]{:S(2)}) collective-permute-start(f32[8,512]{1,0:T(8,128)S(1)} %get-tuple-element.21), channel_id=1, source_target_pairs={{0,64},{16,80},{32,96},{48,112},{64,0},{80,16},{96,32},{112,48},{1... | collective-permute-start | bytes 49160 | tf_op jit(solution)/shard_map/ppermute | solution.py:624
  13.2 0.0 collective-permute-done.refs_7_
  13.2 0.0 collective-permute-done.1.refs_8_
  13.2 2.2 %collective-permute-done.2.refs_9_ = f32[8,512]{1,0:T(8,128)S(1)} collective-permute-done((f32[8,512]{1,0:T(8,128)S(1)}, f32[8,512]{1,0:T(8,128)S(1)}, u32[]{:S(2)}, u32[]{:S(2)}) %collective-permute-start.2) | collective-permute-done | bytes 16416 | tf_op jit(solution)/shard_map/ppermute | solution.py:624
  15.4 15.3 %cell_sums.1 = (f32[2,512]{1,0:T(2,128)S(1)}, f32[2,512]{1,0:T(2,128)S(1)}, f32[2,512]{1,0:T(2,128)S(1)}, f32[2,512]{1,0:T(2,128)S(1)}, f32[30,16384]{1,0:T(8,128)}, /*index=5*/f32[30,16384]{1,0:T(8,128)}) custom-call(s32[512,128]{1,0:T(8,128)} %bitcast.13, f32[512,128]{1,0:T(8,128)} %bitcast.14, f32[30,16384]{1,0:T(8,128)} %refs_2_.1, f32[30,16384]{1,0:T(8,128)} %refs_3_.1, ...), custom_call_target="tpu_custom_call" | custom-call | tf_op jit(solution)/shard_map/cell_sums/pallas_call | solution.py:536
  30.8 0.1 collective-permute-start.3
  30.9 1.9 %collective-permute-start.4 = (f32[2,512]{1,0:T(2,128)S(1)}, f32[2,512]{1,0:T(2,128)S(1)}, u32[]{:S(2)}, u32[]{:S(2)}) collective-permute-start(f32[2,512]{1,0:T(2,128)S(1)} %get-tuple-element.24), channel_id=1, source_target_pairs={{0,15},{1,2},{2,1},{3,4},{4,3},{5,6},{6,5},{7,8},{8,7},{9,10},{10,... | collective-permute-start | bytes 12296 | tf_op jit(solution)/shard_map/ppermute | solution.py:623
  32.8 3.0 %collective-permute-start.5 = (f32[2,512]{1,0:T(2,128)S(1)}, f32[2,512]{1,0:T(2,128)S(1)}, u32[]{:S(2)}, u32[]{:S(2)}) collective-permute-start(f32[2,512]{1,0:T(2,128)S(1)} %get-tuple-element.25), channel_id=1, source_target_pairs={{0,64},{16,80},{32,96},{48,112},{64,0},{80,16},{96,32},{112,48},{1... | collective-permute-start | bytes 12296 | tf_op jit(solution)/shard_map/ppermute | solution.py:624
  35.8 0.0 collective-permute-done.3.p1
  35.8 2.1 %collective-permute-done.4.p2 = f32[2,512]{1,0:T(2,128)S(1)} collective-permute-done((f32[2,512]{1,0:T(2,128)S(1)}, f32[2,512]{1,0:T(2,128)S(1)}, u32[]{:S(2)}, u32[]{:S(2)}) %collective-permute-start.4) | collective-permute-done | bytes 4128 | tf_op jit(solution)/shard_map/ppermute | solution.py:623
  37.9 0.0 collective-permute-done.5.p3
  37.9 1.1 %row_sums.1 = (f32[80,128]{1,0:T(8,128)}, f32[80,128]{1,0:T(8,128)}) custom-call(s32[16,128]{1,0:T(8,128)S(1)} %get-tuple-element.17.index, f32[2,512]{1,0:T(2,128)S(1)} %get-tuple-element.22.p0, f32[2,512]{1,0:T(2,128)S(1)} %collective-permute-done.3.p1, f32[2,512]{1,0:T(2,128)S(1)} %collective-permute-done.4.p2, f32[2,512]{1,0:T(2,128)S(1)} %collective-permute-done.5.p3), custom_call_target="tpu_custom_call" | custom-call | tf_op jit(solution)/shard_map/row_sums/pallas_call | solution.py:594
Async XLA Ops:
  3.1 10.1 %collective-permute-start = (f32[8,512]{1,0:T(8,128)S(1)}, f32[8,512]{1,0:T(8,128)S(1)}, u32[]{:S(2)}, u32[]{:S(2)}) collective-permute-start(f32[8,512]{1,0:T(8,128)S(1)} %get-tuple-element.19), channel_id=1, source_target_pairs={{0,1},{1,0},{2,3},{3,2},{4,5},{5,4},{6,7},{7,6},{8,9},{9,8},{10,11... | collective-permute-start | bytes 49160 | tf_op jit(solution)/shard_map/ppermute | solution.py:622
  5.2 8.0 %collective-permute-start.1 = (f32[8,512]{1,0:T(8,128)S(1)}, f32[8,512]{1,0:T(8,128)S(1)}, u32[]{:S(2)}, u32[]{:S(2)}) collective-permute-start(f32[8,512]{1,0:T(8,128)S(1)} %get-tuple-element.20), channel_id=1, source_target_pairs={{0,15},{1,2},{2,1},{3,4},{4,3},{5,6},{6,5},{7,8},{8,7},{9,10},{10,... | collective-permute-start | bytes 49160 | tf_op jit(solution)/shard_map/ppermute | solution.py:623
  10.2 5.2 %collective-permute-start.2 = (f32[8,512]{1,0:T(8,128)S(1)}, f32[8,512]{1,0:T(8,128)S(1)}, u32[]{:S(2)}, u32[]{:S(2)}) collective-permute-start(f32[8,512]{1,0:T(8,128)S(1)} %get-tuple-element.21), channel_id=1, source_target_pairs={{0,64},{16,80},{32,96},{48,112},{64,0},{80,16},{96,32},{112,48},{1... | collective-permute-start | bytes 49160 | tf_op jit(solution)/shard_map/ppermute | solution.py:624
  30.8 5.0 %collective-permute-start.3 = (f32[2,512]{1,0:T(2,128)S(1)}, f32[2,512]{1,0:T(2,128)S(1)}, u32[]{:S(2)}, u32[]{:S(2)}) collective-permute-start(f32[2,512]{1,0:T(2,128)S(1)} %get-tuple-element.23), channel_id=1, source_target_pairs={{0,1},{1,0},{2,3},{3,2},{4,5},{5,4},{6,7},{7,6},{8,9},{9,8},{10,11... | collective-permute-start | bytes 12296 | tf_op jit(solution)/shard_map/ppermute | solution.py:622
  30.9 7.0 %collective-permute-start.4 = (f32[2,512]{1,0:T(2,128)S(1)}, f32[2,512]{1,0:T(2,128)S(1)}, u32[]{:S(2)}, u32[]{:S(2)}) collective-permute-start(f32[2,512]{1,0:T(2,128)S(1)} %get-tuple-element.24), channel_id=1, source_target_pairs={{0,15},{1,2},{2,1},{3,4},{4,3},{5,6},{6,5},{7,8},{8,7},{9,10},{10,... | collective-permute-start | bytes 12296 | tf_op jit(solution)/shard_map/ppermute | solution.py:623
  32.8 5.1 %collective-permute-start.5 = (f32[2,512]{1,0:T(2,128)S(1)}, f32[2,512]{1,0:T(2,128)S(1)}, u32[]{:S(2)}, u32[]{:S(2)}) collective-permute-start(f32[2,512]{1,0:T(2,128)S(1)} %get-tuple-element.25), channel_id=1, source_target_pairs={{0,64},{16,80},{32,96},{48,112},{64,0},{80,16},{96,32},{112,48},{1... | collective-permute-start | bytes 12296 | tf_op jit(solution)/shard_map/ppermute | solution.py:624
